TPU v7x, 512 devices: a whole 4x8x8 slice. The times are simulated.
512 devices in a mesh: seq: 128 (over y, z_lo, x), chan: 4 (over z_hi, core).
Axes of the slice: x: 4, y: 8, z: 8 (z_hi: 2, z_lo: 4; z = z_hi * 4 + z_lo), core: 2. Of those that a mesh axis runs over, the one named last changes fastest.
Arguments:
- gate_in: bfloat16 [128, 16384], P('chan', 'seq'), may hold values from -6 to 6
- value_in: bfloat16 [128, 16384], P('chan', 'seq'), may hold values from -6 to 6
- out_gate: bfloat16 [128, 16384], P('chan', 'seq'), may hold values from -6 to 6
- filter_taps: bfloat16 [128, 16384], P('chan', 'seq'), may hold values from -0.046875 to 0.046875
- out_weight: bfloat16 [128, 8192], P(None, 'chan'), may hold values from -0.0625 to 0.0625
- out_grad: bfloat16 [16384, 8192], P('seq', 'chan'), may hold values from -6 to 6
Outputs:
- grad_gate: bfloat16 [128, 16384], P('chan', 'seq')
- grad_value: bfloat16 [128, 16384], P('chan', 'seq')
- grad_outgate: bfloat16 [128, 16384], P('chan', 'seq')
- grad_taps: float32 [128, 16384], P('chan', 'seq')
All inputs are finite; a program needn't handle non-finite values.
Results may differ from a plain program's by a relative error of at most 0.011.
Values sent between devices are 32-bit elements; how exact they have to be, the bound alone decides.
No kernel may reach another device: no remote copies, remote signals or barrier semaphores. Data moves between devices by JAX's collectives and lax.ppermute only.
A program may use at most 64 MiB of HBM per device.

v0:
```python
import math

import jax
import jax.numpy as jnp
from jax import lax
from jax.sharding import PartitionSpec as P


def along_last(values, matrix):
    return jnp.einsum(
        "...m,mk->...k",
        values,
        matrix,
        precision=lax.Precision.HIGHEST,
        preferred_element_type=jnp.float32,
    )


def phase_table(row_count, col_count, modulus, direction):
    row_index = jnp.arange(row_count, dtype=jnp.int32)[:, None]
    col_index = jnp.arange(col_count, dtype=jnp.int32)[None, :]
    phase = (row_index * col_index % modulus).astype(jnp.float32) * (2.0 * math.pi / modulus)
    return (jnp.cos(phase), direction * jnp.sin(phase))


def outer_twiddle(first_index, second_index, modulus, direction):
    product = first_index[:, None] * second_index[None, :] % modulus
    phase = product.astype(jnp.float32) * (2.0 * math.pi / modulus)
    return (jnp.cos(phase), direction * jnp.sin(phase))


def complex_product(left_re, left_im, right_re, right_im):
    return (left_re * right_re - left_im * right_im, left_re * right_im + left_im * right_re)


def dense_transform(real_part, imag_part, direction):
    order_len = real_part.shape[-1]
    cos_table, sin_table = phase_table(order_len, order_len, order_len, direction)
    out_re = along_last(real_part, cos_table) - along_last(imag_part, sin_table)
    out_im = along_last(real_part, sin_table) + along_last(imag_part, cos_table)
    return (out_re, out_im)


def held_frequencies(seq_place):
    offsets = jnp.arange(2, dtype=jnp.int32)
    held_freq = 2 * seq_place + offsets
    return held_freq


def to_spectrum(signal):
    stack_count, channels, tok_rows = signal.shape
    seq_count = lax.axis_size("seq")
    seq_place = lax.axis_index("seq")
    full_length = 2 * tok_rows * seq_count
    slice_len = tok_rows // seq_count
    row_blocks = lax.all_to_all(
        signal[:, :, None, :], "seq", split_axis=3, concat_axis=2, tiled=True
    )
    cos_table, sin_table = phase_table(seq_count, 2 * seq_count, 2 * seq_count, -1.0)
    real_part = jnp.einsum(
        "scpm,pk->sckm",
        row_blocks,
        cos_table,
        precision=lax.Precision.HIGHEST,
        preferred_element_type=jnp.float32,
    )
    imag_part = jnp.einsum(
        "scpm,pk->sckm",
        row_blocks,
        sin_table,
        precision=lax.Precision.HIGHEST,
        preferred_element_type=jnp.float32,
    )
    positions = seq_place * slice_len + jnp.arange(slice_len, dtype=jnp.int32)
    wave_re, wave_im = outer_twiddle(
        jnp.arange(2 * seq_count, dtype=jnp.int32), positions, full_length, -1.0
    )
    real_part, imag_part = complex_product(real_part, imag_part, wave_re, wave_im)
    packed = lax.all_to_all(
        jnp.stack([real_part, imag_part]), "seq", split_axis=3, concat_axis=4, tiled=True
    )
    real_part, imag_part = (packed[0], packed[1])
    return dense_transform(real_part, imag_part, -1.0)


def from_spectrum(spec_re, spec_im):
    stack_count, channels, pair_count, tok_rows = spec_re.shape
    seq_count = lax.axis_size("seq")
    seq_place = lax.axis_index("seq")
    full_length = 2 * tok_rows * seq_count
    real_part, imag_part = dense_transform(spec_re, spec_im, 1.0)
    wave_re, wave_im = outer_twiddle(
        held_frequencies(seq_place), jnp.arange(tok_rows, dtype=jnp.int32), full_length, 1.0
    )
    real_part, imag_part = complex_product(real_part, imag_part, wave_re, wave_im)
    col_blocks = lax.all_to_all(
        jnp.stack([real_part, imag_part]), "seq", split_axis=4, concat_axis=3, tiled=True
    )
    cos_table, sin_table = phase_table(2 * seq_count, seq_count, 2 * seq_count, 1.0)
    row_blocks = jnp.einsum(
        "sckm,kp->scpm",
        col_blocks[0],
        cos_table,
        precision=lax.Precision.HIGHEST,
        preferred_element_type=jnp.float32,
    )
    row_blocks = row_blocks - jnp.einsum(
        "sckm,kp->scpm",
        col_blocks[1],
        sin_table,
        precision=lax.Precision.HIGHEST,
        preferred_element_type=jnp.float32,
    )
    row_blocks = row_blocks * (1.0 / full_length)
    time_block = lax.all_to_all(row_blocks, "seq", split_axis=2, concat_axis=3, tiled=True).reshape(
        stack_count, channels, tok_rows
    )
    return time_block


def local(gate_in, value_in, out_gate, filter_taps, out_weight, out_grad):
    channels, tok_rows = gate_in.shape
    total_rows = tok_rows * lax.axis_size("seq")
    gated_input = (gate_in.astype(jnp.float32) * value_in.astype(jnp.float32)).astype(jnp.bfloat16)
    forward_re, forward_im = to_spectrum(
        jnp.stack([gated_input.astype(jnp.float32), filter_taps.astype(jnp.float32)])
    )
    gated_re, gated_im = (forward_re[0], forward_im[0])
    taps_re, taps_im = (forward_re[1], forward_im[1])
    conv_re, conv_im = complex_product(gated_re, gated_im, taps_re, taps_im)
    conv_out = from_spectrum(conv_re[None], conv_im[None])[0]
    grad_mix = lax.psum_scatter(
        lax.dot_general(
            out_weight, out_grad, (((1,), (1,)), ((), ())), preferred_element_type=jnp.float32
        ),
        "chan",
        scatter_dimension=0,
        tiled=True,
    )
    grad_outgate = (grad_mix * conv_out).astype(jnp.bfloat16)
    grad_conv = (grad_mix * out_gate.astype(jnp.float32)).astype(jnp.bfloat16)
    back_re, back_im = to_spectrum(grad_conv.astype(jnp.float32)[None])
    grad_re, grad_im = (back_re[0], back_im[0])
    input_re, input_im = complex_product(grad_re, grad_im, taps_re, -taps_im)
    lag_re, lag_im = complex_product(grad_re, grad_im, gated_re, -gated_im)
    results = from_spectrum(jnp.stack([input_re, lag_re]), jnp.stack([input_im, lag_im]))
    grad_input = results[0]
    grad_gate = (grad_input * value_in.astype(jnp.float32)).astype(jnp.bfloat16)
    grad_value = (grad_input * gate_in.astype(jnp.float32)).astype(jnp.bfloat16)
    grad_taps = results[1] * (1.0 / math.sqrt(total_rows))
    return (grad_gate, grad_value, grad_outgate, grad_taps)


def solution(mesh):
    in_specs = (
        P("chan", "seq"),
        P("chan", "seq"),
        P("chan", "seq"),
        P("chan", "seq"),
        P(None, "chan"),
        P("seq", "chan"),
    )
    out_specs = (P("chan", "seq"), P("chan", "seq"), P("chan", "seq"), P("chan", "seq"))
    return jax.shard_map(local, mesh=mesh, in_specs=in_specs, out_specs=out_specs, check_vma=False)
```

profile of v0, /device:TPU:2, one launch (start us, length us, event | category | flops | bytes accessed | tf_op | source)
XLA Modules:
  0.0 217.4 jit_solution(6279526798366685313)
XLA Ops:
  7.2 1.0 copy-done
  8.2 2.0 fusion.236
  12.4 16.9 %all-to-all-start.2 = ((f32[2,32,1,128]{1,0,2,3:T(2,128)}), f32[2,32,1,128]{1,0,2,3:T(2,128)S(1)}, u32[]{:S(2)}, u32[]{:S(2)}) async-start(f32[2,32,1,128]{1,0,2,3:T(2,128)} %copy.50), calls=%async_computation.3 | async-start | bytes 262144 | tf_op jit(solution)/shard_map/all_to_all | solution.py:56
  29.5 11.5 %all-to-all-done.2 = f32[2,32,1,128]{1,0,2,3:T(2,128)S(1)} async-done(((f32[2,32,1,128]{1,0,2,3:T(2,128)}), f32[2,32,1,128]{1,0,2,3:T(2,128)S(1)}, u32[]{:S(2)}, u32[]{:S(2)}) %all-to-all-start.2) | async-done | bytes 32800 | tf_op jit(solution)/shard_map/all_to_all | solution.py:56
  41.0 14.8 %reduce-scatter.2.cloned.1.call-done = f32[32,128]{1,0:T(8,128)} async-done(((f32[128,128]{1,0:T(8,128)}), f32[32,128]{1,0:T(8,128)}) %reduce-scatter.2.cloned.1.call-update) | async-done | bytes 16400 | tf_op jit(solution)/shard_map/reduce_scatter | solution.py:132
  57.3 11.6 %all-to-all-start = ((f32[1,32,1,128]{1,2,0,3:T(1,128)}), f32[1,32,1,128]{1,2,0,3:T(1,128)S(1)}, u32[]{:S(2)}, u32[]{:S(2)}) async-start(f32[1,32,1,128]{1,2,0,3:T(1,128)} %copy.46), calls=%async_computation.1 | async-start | bytes 131072 | tf_op jit(solution)/shard_map/all_to_all | solution.py:56
  69.6 10.6 %all-to-all-done = f32[1,32,1,128]{1,2,0,3:T(1,128)S(1)} async-done(((f32[1,32,1,128]{1,2,0,3:T(1,128)}), f32[1,32,1,128]{1,2,0,3:T(1,128)S(1)}, u32[]{:S(2)}, u32[]{:S(2)}) %all-to-all-start) | async-done | bytes 16416 | tf_op jit(solution)/shard_map/all_to_all | solution.py:56
  82.3 1.5 reduce
  84.8 6.5 %all-to-all-start.1 = ((f32[128,1,128]{2,1,0:T(1,128)}), f32[128,1,128]{2,1,0:T(1,128)S(1)}, u32[]{:S(2)}, u32[]{:S(2)}) async-start(f32[128,1,128]{2,1,0:T(1,128)} %reshape.211), calls=%async_computation.2 | async-start | bytes 131072 | tf_op jit(solution)/shard_map/all_to_all | solution.py:79
  92.3 1.2 reshape.213
  93.5 9.1 %all-to-all-done.1 = f32[128,1,128]{2,1,0:T(1,128)S(1)} async-done(((f32[128,1,128]{2,1,0:T(1,128)}), f32[128,1,128]{2,1,0:T(1,128)S(1)}, u32[]{:S(2)}, u32[]{:S(2)}) %all-to-all-start.1) | async-done | bytes 65568 | tf_op jit(solution)/shard_map/all_to_all | solution.py:79
  102.7 6.8 %all-to-all-start.3 = ((f32[128,1,256]{2,1,0:T(1,128)}), f32[128,1,256]{2,1,0:T(1,128)S(1)}, u32[]{:S(2)}, u32[]{:S(2)}) async-start(f32[128,1,256]{2,1,0:T(1,128)} %reshape.213), calls=%async_computation.4 | async-start | bytes 262144 | tf_op jit(solution)/shard_map/all_to_all | solution.py:79
  112.2 9.1 %all-to-all-done.3 = f32[128,1,256]{2,1,0:T(1,128)S(1)} async-done(((f32[128,1,256]{2,1,0:T(1,128)}), f32[128,1,256]{2,1,0:T(1,128)S(1)}, u32[]{:S(2)}, u32[]{:S(2)}) %all-to-all-start.3) | async-done | bytes 131104 | tf_op jit(solution)/shard_map/all_to_all | solution.py:79
  121.4 1.0 reduce.2
  128.3 6.5 %all-to-all-start.6 = ((f32[128,1,128]{2,1,0:T(1,128)}), f32[128,1,128]{2,1,0:T(1,128)S(1)}, u32[]{:S(2)}, u32[]{:S(2)}) async-start(f32[128,1,128]{2,1,0:T(1,128)} %reshape.217), calls=%async_computation.7 | async-start | bytes 131072 | tf_op jit(solution)/shard_map/all_to_all | solution.py:96
  136.7 9.6 %all-to-all-done.6 = f32[128,1,128]{2,1,0:T(1,128)S(1)} async-done(((f32[128,1,128]{2,1,0:T(1,128)}), f32[128,1,128]{2,1,0:T(1,128)S(1)}, u32[]{:S(2)}, u32[]{:S(2)}) %all-to-all-start.6) | async-done | bytes 65568 | tf_op jit(solution)/shard_map/all_to_all | solution.py:96
  149.6 6.5 %all-to-all-start.7 = ((f32[1,32,128,1]{1,3,0,2:T(1,128)}), f32[1,32,128,1]{1,3,0,2:T(1,128)S(1)}, u32[]{:S(2)}, u32[]{:S(2)}) async-start(f32[1,32,128,1]{1,3,0,2:T(1,128)} %copy.63), calls=%async_computation.8 | async-start | bytes 131072 | tf_op jit(solution)/shard_map/all_to_all | solution.py:115
  156.5 1.2 reshape.215
  157.7 9.8 %all-to-all-done.7 = f32[1,32,128,1]{1,3,0,2:T(1,128)S(1)} async-done(((f32[1,32,128,1]{1,3,0,2:T(1,128)}), f32[1,32,128,1]{1,3,0,2:T(1,128)S(1)}, u32[]{:S(2)}, u32[]{:S(2)}) %all-to-all-start.7) | async-done | bytes 16416 | tf_op jit(solution)/shard_map/all_to_all | solution.py:115
  167.6 6.6 %all-to-all-start.4 = ((f32[128,1,256]{2,1,0:T(1,128)}), f32[128,1,256]{2,1,0:T(1,128)S(1)}, u32[]{:S(2)}, u32[]{:S(2)}) async-start(f32[128,1,256]{2,1,0:T(1,128)} %reshape.215), calls=%async_computation.5 | async-start | bytes 262144 | tf_op jit(solution)/shard_map/all_to_all | solution.py:96
  174.3 11.7 %all-to-all-done.4 = f32[128,1,256]{2,1,0:T(1,128)S(1)} async-done(((f32[128,1,256]{2,1,0:T(1,128)}), f32[128,1,256]{2,1,0:T(1,128)S(1)}, u32[]{:S(2)}, u32[]{:S(2)}) %all-to-all-start.4) | async-done | bytes 131104 | tf_op jit(solution)/shard_map/all_to_all | solution.py:96
  186.0 1.0 reduce.3
  190.5 6.7 %all-to-all-start.5 = ((f32[2,32,128,1]{1,3,0,2:T(1,128)}), f32[2,32,128,1]{1,3,0,2:T(1,128)S(1)}, u32[]{:S(2)}, u32[]{:S(2)}) async-start(f32[2,32,128,1]{1,3,0,2:T(1,128)} %copy.60), calls=%async_computation.6 | async-start | bytes 262144 | tf_op jit(solution)/shard_map/all_to_all | solution.py:115
  197.9 11.2 %all-to-all-done.5 = f32[2,32,128,1]{1,3,0,2:T(1,128)S(1)} async-done(((f32[2,32,128,1]{1,3,0,2:T(1,128)}), f32[2,32,128,1]{1,3,0,2:T(1,128)S(1)}, u32[]{:S(2)}, u32[]{:S(2)}) %all-to-all-start.5) | async-done | bytes 32800 | tf_op jit(solution)/shard_map/all_to_all | solution.py:115
  (79 shorter events, 28.4 us)
Async XLA Ops:
  7.2 1.0 copy-start
  7.2 48.7 %reduce-scatter.2.cloned.1.call-start = ((), (), s32[]{:S(2)}) async-start(), calls=%async_computation.9 | async-start | bytes 81920 | tf_op jit(solution)/shard_map/reduce_scatter | solution.py:132
  10.2 0.7 copy-start.2
  10.2 0.7 copy-start.3
  10.9 0.7 copy-start.5
  12.4 28.5 %all-to-all-start.2 = ((f32[2,32,1,128]{1,0,2,3:T(2,128)}), f32[2,32,1,128]{1,0,2,3:T(2,128)S(1)}, u32[]{:S(2)}, u32[]{:S(2)}) async-start(f32[2,32,1,128]{1,0,2,3:T(2,128)} %copy.50), calls=%async_computation.3 | async-start | bytes 262144 | tf_op jit(solution)/shard_map/all_to_all | solution.py:56
  29.4 26.4 %copy-start.4 = (bf16[32,128]{1,0:T(8,128)(2,1)S(1)}, bf16[32,128]{1,0:T(8,128)(2,1)}, u32[]{:S(2)}) copy-start(bf16[32,128]{1,0:T(8,128)(2,1)} %param.8) | copy-start | bytes 24580
  57.3 22.9 %all-to-all-start = ((f32[1,32,1,128]{1,2,0,3:T(1,128)}), f32[1,32,1,128]{1,2,0,3:T(1,128)S(1)}, u32[]{:S(2)}, u32[]{:S(2)}) async-start(f32[1,32,1,128]{1,2,0,3:T(1,128)} %copy.46), calls=%async_computation.1 | async-start | bytes 131072 | tf_op jit(solution)/shard_map/all_to_all | solution.py:56
  84.8 17.9 %all-to-all-start.1 = ((f32[128,1,128]{2,1,0:T(1,128)}), f32[128,1,128]{2,1,0:T(1,128)S(1)}, u32[]{:S(2)}, u32[]{:S(2)}) async-start(f32[128,1,128]{2,1,0:T(1,128)} %reshape.211), calls=%async_computation.2 | async-start | bytes 131072 | tf_op jit(solution)/shard_map/all_to_all | solution.py:79
  102.7 18.7 %all-to-all-start.3 = ((f32[128,1,256]{2,1,0:T(1,128)}), f32[128,1,256]{2,1,0:T(1,128)S(1)}, u32[]{:S(2)}, u32[]{:S(2)}) async-start(f32[128,1,256]{2,1,0:T(1,128)} %reshape.213), calls=%async_computation.4 | async-start | bytes 262144 | tf_op jit(solution)/shard_map/all_to_all | solution.py:79
  128.3 17.9 %all-to-all-start.6 = ((f32[128,1,128]{2,1,0:T(1,128)}), f32[128,1,128]{2,1,0:T(1,128)S(1)}, u32[]{:S(2)}, u32[]{:S(2)}) async-start(f32[128,1,128]{2,1,0:T(1,128)} %reshape.217), calls=%async_computation.7 | async-start | bytes 131072 | tf_op jit(solution)/shard_map/all_to_all | solution.py:96
  149.6 17.9 %all-to-all-start.7 = ((f32[1,32,128,1]{1,3,0,2:T(1,128)}), f32[1,32,128,1]{1,3,0,2:T(1,128)S(1)}, u32[]{:S(2)}, u32[]{:S(2)}) async-start(f32[1,32,128,1]{1,3,0,2:T(1,128)} %copy.63), calls=%async_computation.8 | async-start | bytes 131072 | tf_op jit(solution)/shard_map/all_to_all | solution.py:115
  167.6 18.4 %all-to-all-start.4 = ((f32[128,1,256]{2,1,0:T(1,128)}), f32[128,1,256]{2,1,0:T(1,128)S(1)}, u32[]{:S(2)}, u32[]{:S(2)}) async-start(f32[128,1,256]{2,1,0:T(1,128)} %reshape.215), calls=%async_computation.5 | async-start | bytes 262144 | tf_op jit(solution)/shard_map/all_to_all | solution.py:96
  190.5 6.7 %copy-start.1 = (f32[32,128]{1,0:T(8,128)S(1)}, f32[32,128]{1,0:T(8,128)}, u32[]{:S(2)}) copy-start(f32[32,128]{1,0:T(8,128)} %reduce-scatter.2.cloned.1.call-done) | copy-start | bytes 49156
  190.5 18.5 %all-to-all-start.5 = ((f32[2,32,128,1]{1,3,0,2:T(1,128)}), f32[2,32,128,1]{1,3,0,2:T(1,128)S(1)}, u32[]{:S(2)}, u32[]{:S(2)}) async-start(f32[2,32,128,1]{1,3,0,2:T(1,128)} %copy.60), calls=%async_computation.6 | async-start | bytes 262144 | tf_op jit(solution)/shard_map/all_to_all | solution.py:115
Sparse Core Ops, SparseCore 0:
  11.0 44.8 reduce-scatter.1
where the time goes:
time: 218 us; the launch traced here: 217 us
  waiting for transfers between devices  97.6 us (45%)
  starting transfers between devices  68.2 us (31%)
  matrix products  15.2 us (7%)
  local copies, waits for them, and re-layouts  14.6 us (7%)
  between operations  14.5 us (7%)
  other arithmetic  7.33 us (3%)
    all_to_all x2, starting transfers between devices, to_spectrum(): lax.all_to_all(signal[:, :, None, :], 'seq', split_axis=3, concat_axis=2,...  28.5 us
    all_to_all x2, waiting for transfers between devices, to_spectrum(): lax.all_to_all(signal[:, :, None, :], 'seq', split_axis=3, concat_axis=2,...  22.1 us
    all_to_all x2, waiting for transfers between devices, from_spectrum(): lax.all_to_all(jnp.stack([real_part, imag_part]), 'seq', split_axis=4, co...  21.3 us
    all_to_all x2, waiting for transfers between devices, from_spectrum(): lax.all_to_all(row_blocks, 'seq', split_axis=2, concat_axis=3, tiled=True)  21 us
    all_to_all x2, waiting for transfers between devices, to_spectrum(): lax.all_to_all(jnp.stack([real_part, imag_part]), 'seq', split_axis=3, co...  18.3 us
    reduce_scatter x1, waiting for transfers between devices, local(): lax.psum_scatter(lax.dot_general(out_weight, out_grad, (((1,), (1,)), (()...  14.8 us
    all_to_all x2, starting transfers between devices, to_spectrum(): lax.all_to_all(jnp.stack([real_part, imag_part]), 'seq', split_axis=3, co...  13.3 us
    all_to_all x2, starting transfers between devices, from_spectrum(): lax.all_to_all(row_blocks, 'seq', split_axis=2, concat_axis=3, tiled=True)  13.2 us
  transfers between devices with their start and end apart: 9, of which 9 were waited for; matrix products, arithmetic and copies ran while one was open for 5% of the time, Pallas kernels for 0%

commit v1 on v0

v1 whole, which is shorter than its diff:
```python
import math

import jax
import jax.numpy as jnp
from jax import lax
from jax.experimental import pallas as pl
from jax.experimental.pallas import tpu as pltpu
from jax.sharding import Mesh
from jax.sharding import PartitionSpec as P

BLOCK = 128
SHARE = 32
GROUP = 8
SEQ = ("y_hi", "y_lo", "z", "x")
OWNERS = ("y_lo", "z", "x")
CHAN = ("z_hi", "core")


def correlate_kernel(start_ref, signal_ref, out_ref, gated_pad, grad_pad):
    start = start_ref[0]
    zeros = jnp.zeros((BLOCK, BLOCK), jnp.float32)
    grad_pad[:BLOCK, :] = signal_ref[:, :BLOCK]
    grad_pad[BLOCK:, :] = zeros
    gated_pad[:BLOCK, :] = zeros
    gated_pad[BLOCK:, :] = signal_ref[:, BLOCK : 2 * BLOCK]
    row = lax.broadcasted_iota(jnp.int32, (BLOCK, BLOCK), 0)
    col = lax.broadcasted_iota(jnp.int32, (BLOCK, BLOCK), 1)
    upper = col >= row

    def rolled(rows, index):
        wide = jnp.broadcast_to(rows[index : index + 1, :], (BLOCK, BLOCK))
        return pltpu.roll(wide, 0, 1, stride=1, stride_axis=0)

    def step(number, carry):
        last_taps, last_gated, conv, corr = carry
        base = pl.multiple_of(number * GROUP, GROUP)
        gated_rows = signal_ref[pl.ds(base, GROUP), BLOCK : 2 * BLOCK]
        taps_rows = signal_ref[pl.ds(base, GROUP), 2 * BLOCK :]
        taps_mats, gated_mats, gated_left, grad_left = [], [], [], []
        for index in range(GROUP):
            this_taps, this_gated = rolled(taps_rows, index), rolled(gated_rows, index)
            taps_mats.append(jnp.where(upper, this_taps, last_taps).astype(jnp.bfloat16))
            gated_mats.append(jnp.where(upper, this_gated, last_gated).astype(jnp.bfloat16))
            last_taps, last_gated = this_taps, this_gated
            block = base + index
            gated_left.append(gated_pad[pl.ds(BLOCK + start - block, SHARE), :])
            grad_left.append(grad_pad[pl.ds(start + block, SHARE), :])
        conv = conv + jnp.dot(
            jnp.concatenate(gated_left, 1).astype(jnp.bfloat16),
            jnp.concatenate(taps_mats, 0),
            preferred_element_type=jnp.float32,
        )
        corr = corr + lax.dot_general(
            jnp.concatenate(grad_left, 1).astype(jnp.bfloat16),
            jnp.concatenate(
                [jnp.concatenate(taps_mats, 1), jnp.concatenate(gated_mats, 1)], 0
            ),
            (((1,), (1,)), ((), ())),
            preferred_element_type=jnp.float32,
        )
        return last_taps, last_gated, conv, corr

    _, _, conv, corr = lax.fori_loop(
        0,
        BLOCK // GROUP,
        step,
        (
            zeros,
            zeros,
            jnp.zeros((SHARE, BLOCK), jnp.float32),
            jnp.zeros((SHARE, 2 * BLOCK), jnp.float32),
        ),
    )
    out_ref[:, :BLOCK] = conv
    out_ref[:, BLOCK:] = corr


def correlate(start, signals):
    return pl.pallas_call(
        correlate_kernel,
        out_shape=jax.ShapeDtypeStruct((SHARE, 3 * BLOCK), jnp.float32),
        in_specs=[
            pl.BlockSpec(memory_space=pltpu.SMEM),
            pl.BlockSpec(memory_space=pltpu.VMEM),
        ],
        out_specs=pl.BlockSpec(memory_space=pltpu.VMEM),
        scratch_shapes=[pltpu.VMEM((2 * BLOCK, BLOCK), jnp.float32)] * 2,
        compiler_params=pltpu.CompilerParams(vmem_limit_bytes=32 * 1024 * 1024),
        cost_estimate=pl.CostEstimate(
            flops=6 * SHARE * BLOCK**3, bytes_accessed=250000, transcendentals=0
        ),
        name="correlate",
    )(start, signals)


def local(gate_in, value_in, out_gate, filter_taps, out_weight, out_grad):
    channels, tok_rows = gate_in.shape
    gate, value = gate_in.astype(jnp.float32), value_in.astype(jnp.float32)
    gated = (gate * value).astype(jnp.bfloat16).astype(jnp.float32)
    taps = filter_taps.astype(jnp.float32)
    partial = lax.dot_general(
        out_weight, out_grad, (((1,), (1,)), ((), ())), preferred_element_type=jnp.float32
    ).reshape(2, 2, channels, tok_rows)
    core, half = lax.axis_index("core"), lax.axis_index("z_hi")
    swap = [(0, 1), (1, 0)]
    kept = jnp.where(core == 0, partial[:, 0], partial[:, 1])
    sent = jnp.where(core == 0, partial[:, 1], partial[:, 0])
    partial = kept + lax.ppermute(sent, "core", swap)
    kept = jnp.where(half == 0, partial[0], partial[1])
    sent = jnp.where(half == 0, partial[1], partial[0])
    grad_mix = kept + lax.ppermute(sent, "z_hi", swap)
    grad_conv = (grad_mix * out_gate.astype(jnp.float32)).astype(jnp.bfloat16)
    signals = jnp.concatenate([grad_conv.astype(jnp.float32), gated, taps], axis=1)
    signals = lax.all_to_all(
        jnp.concatenate([signals] * 4, axis=0), SEQ, split_axis=0, concat_axis=0, tiled=True
    )
    start = (lax.axis_index("y_hi") * SHARE).astype(jnp.int32).reshape(1)
    results = correlate(start, signals)
    results = lax.all_to_all(results, OWNERS, split_axis=0, concat_axis=0, tiled=True)
    conv, grad_input, grad_taps = (
        results[:, :BLOCK],
        results[:, BLOCK : 2 * BLOCK],
        results[:, 2 * BLOCK :],
    )
    grad_outgate = (grad_mix * conv).astype(jnp.bfloat16)
    grad_gate = (grad_input * value).astype(jnp.bfloat16)
    grad_value = (grad_input * gate).astype(jnp.bfloat16)
    return (grad_gate, grad_value, grad_outgate, grad_taps * (1.0 / math.sqrt(BLOCK * BLOCK)))


def solution(mesh):
    fine = Mesh(mesh.devices.reshape(4, 2, 4, 4, 2, 2), SEQ + CHAN)
    rows = P(CHAN, SEQ)
    return jax.shard_map(
        local,
        mesh=fine,
        in_specs=(rows, rows, rows, rows, P(None, CHAN), P(SEQ, CHAN)),
        out_specs=(rows, rows, rows, rows),
        check_vma=False,
    )
```

time: 218 us -> 66.8 us (0.31)
  the two profiles are of different devices: /device:TPU:2 before, /device:TPU:8 now
where the time goes in v1:
time: 66.8 us; the launch traced here: 66.4 us
  starting transfers between devices  26.9 us (40%)
  waiting for transfers between devices  15.4 us (23%)
  blocking collectives  12.1 us (18%)
  Pallas kernels  7.11 us (11%)
  local copies, waits for them, and re-layouts  2.01 us (3%)
  matrix products  1.34 us (2%)
  between operations  0.8 us (1%)
  other arithmetic  0.68 us (1%)
    all_to_all x1, starting transfers between devices, local(): lax.all_to_all(jnp.concatenate([signals] * 4, axis=0), SEQ, split_axis=0,...  14.1 us
    all_to_all x1, waiting for transfers between devices, local(): lax.all_to_all(jnp.concatenate([signals] * 4, axis=0), SEQ, split_axis=0,...  12.6 us
    all_to_all x1, blocking collectives, local(): lax.all_to_all(results, OWNERS, split_axis=0, concat_axis=0, tiled=True)  12.1 us
    ppermute x1, starting transfers between devices, local(): grad_mix = kept + lax.ppermute(sent, 'z_hi', swap)  10.9 us
    pallas_call x1, Pallas kernels, correlate(): pl.pallas_call(correlate_kernel, out_shape=jax.ShapeDtypeStruct((SHARE, 3...  7.11 us
    ppermute x1, starting transfers between devices, local(): partial = kept + lax.ppermute(sent, 'core', swap)  1.92 us
    ppermute x1, waiting for transfers between devices, local(): grad_mix = kept + lax.ppermute(sent, 'z_hi', swap)  1.66 us
    dot_general x1, matrix products, local(): lax.dot_general(out_weight, out_grad, (((1,), (1,)), ((), ())), preferred...  1.34 us
  transfers between devices with their start and end apart: 3, of which 3 were waited for; matrix products, arithmetic and copies ran while one was open for 0% of the time, Pallas kernels for 0%

profile of v1, /device:TPU:8, one launch (start us, length us, event | category | flops | bytes accessed | tf_op | source)
XLA Modules:
  0.0 66.4 jit_solution(15360617782827033683)
XLA Ops:
  0.6 0.0 copy-start
  0.7 1.0 %copy-done = bf16[128,2048]{1,0:T(8,128)(2,1)S(1)} copy-done((bf16[128,2048]{1,0:T(8,128)(2,1)S(1)}, bf16[128,2048]{1,0:T(8,128)(2,1)}, u32[]{:S(2)}) %copy-start) | copy-done | bytes 524312
  1.7 1.3 %fusion.7 = f32[128,128]{1,0:T(8,128)S(1)} fusion(bf16[128,2048]{1,0:T(8,128)(2,1)S(1)} %copy-done, bf16[128,2048]{1,0:T(8,128)(2,1)} %param.11), kind=kOutput, calls=%fused_computation.20 | convolution fusion | flops 67108864 | bytes 1114112 | tf_op jit(solution)/shard_map/dot_general | solution.py:101
  3.0 1.9 %collective-permute-start = (f32[2,32,128]{2,1,0:T(8,128)S(1)}, f32[2,32,128]{2,1,0:T(8,128)S(1)}, u32[]{:S(2)}, u32[]{:S(2)}) collective-permute-start(f32[2,32,128]{2,1,0:T(8,128)S(1)} %select_bitcast_fusion), channel_id=1, source_target_pairs={{0,1},{1,0},{2,3},{3,2},{4,5},{5,4},{6,7},{7,6},{8,9},{9,8},{10,11... | collective-permute-start | bytes 98312 | tf_op jit(solution)/shard_map/ppermute | solution.py:108
  5.0 1.2 %collective-permute-done = f32[2,32,128]{2,1,0:T(8,128)S(1)} collective-permute-done((f32[2,32,128]{2,1,0:T(8,128)S(1)}, f32[2,32,128]{2,1,0:T(8,128)S(1)}, u32[]{:S(2)}, u32[]{:S(2)}) %collective-permute-start) | collective-permute-done | bytes 32800 | tf_op jit(solution)/shard_map/ppermute | solution.py:108
  6.2 0.0 copy-start.1
  6.2 0.0 copy-start.2
  6.2 0.0 copy-start.4
  6.2 10.9 %collective-permute-start.1 = (f32[32,128]{1,0:T(8,128)S(1)}, f32[32,128]{1,0:T(8,128)S(1)}, u32[]{:S(2)}, u32[]{:S(2)}) collective-permute-start(f32[32,128]{1,0:T(8,128)S(1)} %select_bitcast_fusion.1), channel_id=1, source_target_pairs={{0,2},{2,0},{1,3},{3,1},{4,6},{6,4},{5,7},{7,5},{8,10},{10,8},{9,1... | collective-permute-start | bytes 49160 | tf_op jit(solution)/shard_map/ppermute | solution.py:111
  17.1 0.0 copy-done.1
  17.1 0.0 copy-done.2
  17.2 0.0 copy-start.3
  17.2 1.7 %collective-permute-done.1 = f32[32,128]{1,0:T(8,128)S(1)} collective-permute-done((f32[32,128]{1,0:T(8,128)S(1)}, f32[32,128]{1,0:T(8,128)S(1)}, u32[]{:S(2)}, u32[]{:S(2)}) %collective-permute-start.1) | collective-permute-done | bytes 16416 | tf_op jit(solution)/shard_map/ppermute | solution.py:111
  18.8 0.0 copy-done.4
  18.8 0.0 copy-done.3
  18.9 0.9 %copy.16 = f32[128,1,384]{2,1,0:T(1,128)} copy(f32[128,1,384]{2,0,1:T(8,128)S(1)} %fusion) | data formatting | bytes 393216 | tf_op jit(solution)/shard_map/all_to_all | solution.py:114
  19.8 14.1 %all-to-all-start = ((f32[128,1,384]{2,1,0:T(1,128)}), f32[128,1,384]{2,1,0:T(1,128)S(1)}, u32[]{:S(2)}, u32[]{:S(2)}) async-start(f32[128,1,384]{2,1,0:T(1,128)} %copy.16), calls=%async_computation | async-start | bytes 393216 | tf_op jit(solution)/shard_map/all_to_all | solution.py:114
  33.9 12.6 %all-to-all-done = f32[128,1,384]{2,1,0:T(1,128)S(1)} async-done(((f32[128,1,384]{2,1,0:T(1,128)}), f32[128,1,384]{2,1,0:T(1,128)S(1)}, u32[]{:S(2)}, u32[]{:S(2)}) %all-to-all-start) | async-done | bytes 196640 | tf_op jit(solution)/shard_map/all_to_all | solution.py:114
  46.5 7.1 %correlate.1 = f32[32,384]{1,0:T(8,128)S(1)} custom-call(s32[1]{0:T(128)} %bitcast.start_ref, f32[128,384]{1,0:T(8,128)S(1)} %bitcast.39), custom_call_target="tpu_custom_call" | custom-call | flops 402653184 | bytes 250000 | tf_op jit(solution)/shard_map/correlate/pallas_call | solution.py:79
  53.6 0.1 copy.17
  53.7 12.1 %all_to_all.27 = f32[32,1,384]{2,1,0:T(1,128)S(1)} all-to-all(f32[32,1,384]{2,1,0:T(1,128)S(1)} %copy.17), channel_id=1, replica_groups=mesh['y_hi'=4,'y_lo'=2,'z'=4,'x'=4,'z_hi'=2,'core'=2] {'y_lo','z','x'}, dimensions={0} | all-to-all | bytes 98304 | tf_op jit(solution)/shard_map/all_to_all | solution.py:119
  65.8 0.6 slice_multiply_fusion
  (8 shorter events, 0.1 us)
Async XLA Ops:
  0.6 1.0 %copy-start = (bf16[128,2048]{1,0:T(8,128)(2,1)S(1)}, bf16[128,2048]{1,0:T(8,128)(2,1)}, u32[]{:S(2)}) copy-start(bf16[128,2048]{1,0:T(8,128)(2,1)} %param.10) | copy-start | bytes 1572868
  3.0 3.1 %collective-permute-start = (f32[2,32,128]{2,1,0:T(8,128)S(1)}, f32[2,32,128]{2,1,0:T(8,128)S(1)}, u32[]{:S(2)}, u32[]{:S(2)}) collective-permute-start(f32[2,32,128]{2,1,0:T(8,128)S(1)} %select_bitcast_fusion), channel_id=1, source_target_pairs={{0,1},{1,0},{2,3},{3,2},{4,5},{5,4},{6,7},{7,6},{8,9},{9,8},{10,11... | collective-permute-start | bytes 98312 | tf_op jit(solution)/shard_map/ppermute | solution.py:108
  6.2 11.0 %copy-start.1 = (bf16[32,128]{1,0:T(8,128)(2,1)S(1)}, bf16[32,128]{1,0:T(8,128)(2,1)}, u32[]{:S(2)}) copy-start(bf16[32,128]{1,0:T(8,128)(2,1)} %param.7) | copy-start | bytes 24580
  6.2 11.0 %copy-start.2 = (bf16[32,128]{1,0:T(8,128)(2,1)S(1)}, bf16[32,128]{1,0:T(8,128)(2,1)}, u32[]{:S(2)}) copy-start(bf16[32,128]{1,0:T(8,128)(2,1)} %param.6) | copy-start | bytes 24580
  6.2 12.6 %copy-start.4 = (bf16[32,128]{1,0:T(8,128)(2,1)S(1)}, bf16[32,128]{1,0:T(8,128)(2,1)}, u32[]{:S(2)}) copy-start(bf16[32,128]{1,0:T(8,128)(2,1)} %param.8) | copy-start | bytes 24580
  6.2 12.6 %collective-permute-start.1 = (f32[32,128]{1,0:T(8,128)S(1)}, f32[32,128]{1,0:T(8,128)S(1)}, u32[]{:S(2)}, u32[]{:S(2)}) collective-permute-start(f32[32,128]{1,0:T(8,128)S(1)} %select_bitcast_fusion.1), channel_id=1, source_target_pairs={{0,2},{2,0},{1,3},{3,1},{4,6},{6,4},{5,7},{7,5},{8,10},{10,8},{9,1... | collective-permute-start | bytes 49160 | tf_op jit(solution)/shard_map/ppermute | solution.py:111
  17.2 1.7 %copy-start.3 = (bf16[32,128]{1,0:T(8,128)(2,1)S(1)}, bf16[32,128]{1,0:T(8,128)(2,1)}, u32[]{:S(2)}) copy-start(bf16[32,128]{1,0:T(8,128)(2,1)} %param.9) | copy-start | bytes 24580
  19.8 26.7 %all-to-all-start = ((f32[128,1,384]{2,1,0:T(1,128)}), f32[128,1,384]{2,1,0:T(1,128)S(1)}, u32[]{:S(2)}, u32[]{:S(2)}) async-start(f32[128,1,384]{2,1,0:T(1,128)} %copy.16), calls=%async_computation | async-start | bytes 393216 | tf_op jit(solution)/shard_map/all_to_all | solution.py:114

commit v2 on v1

v2 whole, which is shorter than its diff:
```python
import jax
import jax.numpy as jnp
import numpy as np
from jax import lax
from jax.experimental import pallas as pl
from jax.experimental.pallas import tpu as pltpu
from jax.sharding import Mesh
from jax.sharding import PartitionSpec as P

SIDE = 128
SHARE = 32
LENGTH = SIDE * SIDE
SEQ = ("y_hi", "y_lo", "z", "x")
OWNERS = ("y_lo", "z", "x")
CHAN = ("z_hi", "core")


def transform_tables():
    index = np.arange(SIDE)
    quarter = 4 * index + 1
    angle = 2 * np.pi * np.outer(quarter, index) / (4 * SIDE)
    rows = np.concatenate([np.cos(angle), -np.sin(angle)], axis=0)
    angle = 2 * np.pi * (np.outer(index, index) % SIDE) / SIDE
    cos, sin = np.cos(angle), np.sin(angle)
    columns = np.block([[cos, -sin], [sin, cos]])
    angle = 2 * np.pi * np.outer(quarter, index) / (4 * LENGTH)
    wave = np.concatenate([np.cos(angle), np.sin(angle)], axis=1)
    table = np.concatenate([columns, rows.T, wave], axis=0)
    return rows.astype(np.float32), table.astype(np.float32)


def product(left, right):
    return jnp.dot(left, right, preferred_element_type=jnp.float32)


def split(values):
    high = values.astype(jnp.bfloat16)
    return high, (values - high.astype(jnp.float32)).astype(jnp.bfloat16)


def wide_product(left, right):
    (left_high, left_low), (right_high, right_low) = left, right
    small = product(left_low, right_high) + product(left_high, right_low)
    return product(left_high, right_high) + small


def convolve_kernel(place_ref, signal_ref, rows_ref, table_ref, out_ref, mix_ref):
    n = SIDE
    own = pl.ds(pl.multiple_of(place_ref[0] * n, n), n)
    share = pl.multiple_of(place_ref[1] * SHARE, SHARE)
    grad_mix = signal_ref[:n, :n] + signal_ref[n:, :n]
    mix_ref[...] = grad_mix
    grad_conv = (grad_mix * signal_ref[own, 3 * n :]).astype(jnp.bfloat16)
    others = signal_ref[own, n : 3 * n].astype(jnp.bfloat16)
    signals = jnp.concatenate([grad_conv, others], axis=1)
    rows_high, rows_low = split(rows_ref[...])
    spread = product(rows_high, signals) + product(rows_low, signals)
    columns = split(table_ref[: 2 * n, :])
    cos, sin = table_ref[3 * n :, :n], table_ref[3 * n :, n:]
    turned = []
    for at in range(3):
        re, im = spread[:n, at * n : (at + 1) * n], spread[n:, at * n : (at + 1) * n]
        turned.append(jnp.concatenate([re * cos + im * sin, im * cos - re * sin], axis=1))
    spectra = wide_product(split(jnp.concatenate(turned, axis=0)), columns)
    grad_re, grad_im = spectra[:n, :n], spectra[:n, n:]
    gated_re, gated_im = spectra[n : 2 * n, :n], spectra[n : 2 * n, n:]
    taps_re, taps_im = spectra[2 * n :, :n], spectra[2 * n :, n:]
    pairs = [
        (gated_re * taps_re - gated_im * taps_im, -(gated_re * taps_im + gated_im * taps_re)),
        (grad_re * taps_re + grad_im * taps_im, grad_re * taps_im - grad_im * taps_re),
        (grad_re * gated_re + grad_im * gated_im, grad_re * gated_im - grad_im * gated_re),
    ]
    pairs = jnp.concatenate([jnp.concatenate(pair, axis=1) for pair in pairs], axis=0)
    back = wide_product(split(pairs), columns)
    turned = []
    for at in range(3):
        re, im = back[at * n : (at + 1) * n, :n], back[at * n : (at + 1) * n, n:]
        turned.append(jnp.concatenate([re * cos + im * sin, re * sin - im * cos], axis=0))
    last = split(table_ref[pl.ds(2 * n + share, SHARE), :])
    results = wide_product(last, split(jnp.concatenate(turned, axis=1))) * (1.0 / LENGTH)
    out_ref[:, :n] = results[:, :n] * mix_ref[pl.ds(share, SHARE), :]
    out_ref[:, n:] = results[:, n:]


def convolve(place, signals):
    rows, table = transform_tables()
    return pl.pallas_call(
        convolve_kernel,
        out_shape=jax.ShapeDtypeStruct((SHARE, 3 * SIDE), jnp.float32),
        in_specs=[pl.BlockSpec(memory_space=pltpu.SMEM)]
        + [pl.BlockSpec(memory_space=pltpu.VMEM)] * 3,
        out_specs=pl.BlockSpec(memory_space=pltpu.VMEM),
        scratch_shapes=[pltpu.VMEM((SIDE, SIDE), jnp.float32)],
        compiler_params=pltpu.CompilerParams(vmem_limit_bytes=32 * 1024 * 1024),
        cost_estimate=pl.CostEstimate(
            flops=400_000_000, bytes_accessed=1_200_000, transcendentals=0
        ),
        name="convolve",
    )(place, signals, jnp.asarray(rows), jnp.asarray(table))


def local(gate_in, value_in, out_gate, filter_taps, out_weight, out_grad):
    channels, tok_rows = gate_in.shape
    gate, value = gate_in.astype(jnp.float32), value_in.astype(jnp.float32)
    gated = (gate * value).astype(jnp.bfloat16).astype(jnp.float32)
    taps, outer = filter_taps.astype(jnp.float32), out_gate.astype(jnp.float32)
    partial = lax.dot_general(
        out_weight, out_grad, (((1,), (1,)), ((), ())), preferred_element_type=jnp.float32
    ).reshape(2, 2, channels, tok_rows)
    core, half = lax.axis_index("core"), lax.axis_index("z_hi")
    kept = jnp.where(core == 0, partial[:, 0], partial[:, 1])
    sent = jnp.where(core == 0, partial[:, 1], partial[:, 0])
    partial = kept + lax.ppermute(sent, "core", [(0, 1), (1, 0)])
    own = [gated, taps, outer]
    signals = [jnp.concatenate([partial[to], *own], axis=1) for to in range(2) for _ in range(4)]
    signals = lax.all_to_all(
        jnp.concatenate(signals, axis=0), ("z_hi",) + SEQ, split_axis=0, concat_axis=0, tiled=True
    )
    place = jnp.stack([half, lax.axis_index("y_hi")]).astype(jnp.int32)
    results = convolve(place, signals)
    results = lax.all_to_all(results, OWNERS, split_axis=0, concat_axis=0, tiled=True)
    grad_outgate, grad_input, grad_taps = (
        results[:, :SIDE],
        results[:, SIDE : 2 * SIDE],
        results[:, 2 * SIDE :],
    )
    grad_gate = (grad_input * value).astype(jnp.bfloat16)
    grad_value = (grad_input * gate).astype(jnp.bfloat16)
    return (grad_gate, grad_value, grad_outgate.astype(jnp.bfloat16), grad_taps * LENGTH**-0.5)


def solution(mesh):
    fine = Mesh(mesh.devices.reshape(4, 2, 4, 4, 2, 2), SEQ + CHAN)
    rows = P(CHAN, SEQ)
    return jax.shard_map(
        local,
        mesh=fine,
        in_specs=(rows, rows, rows, rows, P(None, CHAN), P(SEQ, CHAN)),
        out_specs=(rows, rows, rows, rows),
        check_vma=False,
    )
```

time: 66.8 us -> 66.7 us (level)
  waiting for transfers between devices: 15.4 us -> 21.7 us
  Pallas kernels: 7.11 us -> 1.82 us
  starting transfers between devices: 26.9 us -> 23.3 us
  local copies, waits for them, and re-layouts: 2.01 us -> 3.77 us
    ppermute x2 -> x1, starting transfers between devices: 12.8 us -> 1.92 us  [local(): partial = kept + lax.ppermute(sent, 'core', [(0, 1), (1, 0)])]
    all_to_all x1, waiting for transfers between devices: 12.6 us -> 21.3 us  [local(): lax.all_to_all(jnp.concatenate(signals, axis=0), ('z_hi',) + SEQ, split_a...]
    all_to_all x1, starting transfers between devices: 14.1 us -> 21.3 us  [local(): lax.all_to_all(jnp.concatenate(signals, axis=0), ('z_hi',) + SEQ, split_a...]
    pallas_call x1, Pallas kernels: 7.11 us -> 1.82 us  [convolve(): pl.pallas_call(convolve_kernel, out_shape=jax.ShapeDtypeStruct((SHARE, 3...]
    ppermute x2 -> x1, waiting for transfers between devices: 2.82 us -> 0.43 us  [local(): partial = kept + lax.ppermute(sent, 'core', [(0, 1), (1, 0)])]
    unnamed x12 -> x16, local copies, waits for them, and re-layouts: 1.08 us -> 1.78 us
  transfers between devices with their start and end apart: 3 -> 2, of which waited for: 3 -> 2; matrix products, arithmetic and copies ran while one was open for 0% -> 0% of each run, Pallas kernels for 0% -> 0%
where the time goes in v2:
time: 66.7 us; the launch traced here: 66.3 us
  starting transfers between devices  23.3 us (35%)
  waiting for transfers between devices  21.7 us (33%)
  blocking collectives  12.7 us (19%)
  local copies, waits for them, and re-layouts  3.77 us (6%)
  Pallas kernels  1.82 us (3%)
  matrix products  1.34 us (2%)
  between operations  0.86 us (1%)
  other arithmetic  0.78 us (1%)
    all_to_all x1, starting transfers between devices, local(): lax.all_to_all(jnp.concatenate(signals, axis=0), ('z_hi',) + SEQ, split_a...  21.3 us
    all_to_all x1, waiting for transfers between devices, local(): lax.all_to_all(jnp.concatenate(signals, axis=0), ('z_hi',) + SEQ, split_a...  21.3 us
    all_to_all x1, blocking collectives, local(): lax.all_to_all(results, OWNERS, split_axis=0, concat_axis=0, tiled=True)  12.7 us
    ppermute x1, starting transfers between devices, local(): partial = kept + lax.ppermute(sent, 'core', [(0, 1), (1, 0)])  1.92 us
    pallas_call x1, Pallas kernels, convolve(): pl.pallas_call(convolve_kernel, out_shape=jax.ShapeDtypeStruct((SHARE, 3...  1.82 us
    unnamed x16, local copies, waits for them, and re-layouts  1.78 us
    dot_general x1, matrix products, local(): lax.dot_general(out_weight, out_grad, (((1,), (1,)), ((), ())), preferred...  1.34 us
  transfers between devices with their start and end apart: 2, of which 2 were waited for; matrix products, arithmetic and copies ran while one was open for 0% of the time, Pallas kernels for 0%

profile of v2, /device:TPU:8, one launch (start us, length us, event | category | flops | bytes accessed | tf_op | source)
XLA Modules:
  0.0 66.3 jit_solution(2782888015971207792)
XLA Ops:
  0.6 0.0 copy-start
  0.7 1.0 %copy-done = bf16[128,2048]{1,0:T(8,128)(2,1)S(1)} copy-done((bf16[128,2048]{1,0:T(8,128)(2,1)S(1)}, bf16[128,2048]{1,0:T(8,128)(2,1)}, u32[]{:S(2)}) %copy-start) | copy-done | bytes 524312
  1.7 1.3 %fusion.6 = f32[128,128]{1,0:T(8,128)S(1)} fusion(bf16[128,2048]{1,0:T(8,128)(2,1)S(1)} %copy-done, bf16[128,2048]{1,0:T(8,128)(2,1)} %param.13), kind=kOutput, calls=%fused_computation.32 | convolution fusion | flops 67108864 | bytes 1114112 | tf_op jit(solution)/shard_map/dot_general | solution.py:107
  3.0 0.0 copy-start.3
  3.0 0.0 copy-start.4
  3.1 0.0 copy-start.5
  3.1 1.9 %collective-permute-start = (f32[2,32,128]{2,1,0:T(8,128)S(1)}, f32[2,32,128]{2,1,0:T(8,128)S(1)}, u32[]{:S(2)}, u32[]{:S(2)}) collective-permute-start(f32[2,32,128]{2,1,0:T(8,128)S(1)} %select_bitcast_fusion), channel_id=1, source_target_pairs={{0,1},{1,0},{2,3},{3,2},{4,5},{5,4},{6,7},{7,6},{8,9},{9,8},{10,11... | collective-permute-start | bytes 98312 | tf_op jit(solution)/shard_map/ppermute | solution.py:113
  5.0 0.0 copy-done.3
  5.0 0.0 copy-done.4
  5.0 0.0 copy-done.5
  5.0 0.0 copy-start.6
  5.1 0.7 %copy-done.6 = bf16[32,128]{1,0:T(8,128)(2,1)S(1)} copy-done((bf16[32,128]{1,0:T(8,128)(2,1)S(1)}, bf16[32,128]{1,0:T(8,128)(2,1)}, u32[]{:S(2)}) %copy-start.6) | copy-done | bytes 8216
  5.8 0.4 collective-permute-done
  6.3 1.3 %copy.18 = f32[256,1,512]{2,1,0:T(1,128)} copy(f32[256,1,512]{2,0,1:T(8,128)S(1)} %bitcast.37) | data formatting | bytes 1048576 | tf_op jit(solution)/shard_map/all_to_all | solution.py:116
  7.7 21.3 %all-to-all-start = ((f32[256,1,512]{2,1,0:T(1,128)}), f32[256,1,512]{2,1,0:T(1,128)S(1)}, u32[]{:S(2)}, u32[]{:S(2)}) async-start(f32[256,1,512]{2,1,0:T(1,128)} %copy.18), calls=%async_computation | async-start | bytes 1048576 | tf_op jit(solution)/shard_map/all_to_all | solution.py:116
  29.0 0.1 pad_add_fusion.place_ref
  29.1 21.3 %all-to-all-done = f32[256,1,512]{2,1,0:T(1,128)S(1)} async-done(((f32[256,1,512]{2,1,0:T(1,128)}), f32[256,1,512]{2,1,0:T(1,128)S(1)}, u32[]{:S(2)}, u32[]{:S(2)}) %all-to-all-start) | async-done | bytes 524320 | tf_op jit(solution)/shard_map/all_to_all | solution.py:116
  50.4 0.0 copy-done.1
  50.4 0.0 copy-done.2
  50.4 1.8 %convolve.1 = f32[32,384]{1,0:T(8,128)S(1)} custom-call(s32[2]{0:T(128)S(1)} %pad_add_fusion.place_ref, f32[256,512]{1,0:T(8,128)S(1)} %bitcast.35, f32[256,128]{1,0:T(8,128)S(1)} %copy-done.2, f32[512,256]{1,0:T(8,128)S(1)} %copy-done.1), custom_call_target="tpu_custom_call" | custom-call | flops 400000000 | bytes 1200000 | tf_op jit(solution)/shard_map/convolve/pallas_call | solution.py:87
  52.2 0.1 copy.19
  52.3 12.7 %all_to_all.23 = f32[32,1,384]{2,1,0:T(1,128)S(1)} all-to-all(f32[32,1,384]{2,1,0:T(1,128)S(1)} %copy.19), channel_id=1, replica_groups=mesh['y_hi'=4,'y_lo'=2,'z'=4,'x'=4,'z_hi'=2,'core'=2] {'y_lo','z','x'}, dimensions={0} | all-to-all | bytes 98304 | tf_op jit(solution)/shard_map/all_to_all | solution.py:121
  65.0 0.6 slice.54
  65.6 0.6 slice_multiply_fusion
  (18 shorter events, 0.1 us)
Async XLA Ops:
  0.6 1.0 %copy-start = (bf16[128,2048]{1,0:T(8,128)(2,1)S(1)}, bf16[128,2048]{1,0:T(8,128)(2,1)}, u32[]{:S(2)}) copy-start(bf16[128,2048]{1,0:T(8,128)(2,1)} %param.12) | copy-start | bytes 1572868
  3.0 2.0 %copy-start.3 = (bf16[32,128]{1,0:T(8,128)(2,1)S(1)}, bf16[32,128]{1,0:T(8,128)(2,1)}, u32[]{:S(2)}) copy-start(bf16[32,128]{1,0:T(8,128)(2,1)} %param.9) | copy-start | bytes 24580
  3.0 2.0 %copy-start.4 = (bf16[32,128]{1,0:T(8,128)(2,1)S(1)}, bf16[32,128]{1,0:T(8,128)(2,1)}, u32[]{:S(2)}) copy-start(bf16[32,128]{1,0:T(8,128)(2,1)} %param.8) | copy-start | bytes 24580
  3.1 2.0 %copy-start.5 = (bf16[32,128]{1,0:T(8,128)(2,1)S(1)}, bf16[32,128]{1,0:T(8,128)(2,1)}, u32[]{:S(2)}) copy-start(bf16[32,128]{1,0:T(8,128)(2,1)} %param.10) | copy-start | bytes 24580
  3.1 3.1 %collective-permute-start = (f32[2,32,128]{2,1,0:T(8,128)S(1)}, f32[2,32,128]{2,1,0:T(8,128)S(1)}, u32[]{:S(2)}, u32[]{:S(2)}) collective-permute-start(f32[2,32,128]{2,1,0:T(8,128)S(1)} %select_bitcast_fusion), channel_id=1, source_target_pairs={{0,1},{1,0},{2,3},{3,2},{4,5},{5,4},{6,7},{7,6},{8,9},{9,8},{10,11... | collective-permute-start | bytes 98312 | tf_op jit(solution)/shard_map/ppermute | solution.py:113
  5.0 0.7 %copy-start.6 = (bf16[32,128]{1,0:T(8,128)(2,1)S(1)}, bf16[32,128]{1,0:T(8,128)(2,1)}, u32[]{:S(2)}) copy-start(bf16[32,128]{1,0:T(8,128)(2,1)} %param.11) | copy-start | bytes 24580
  7.7 42.7 %all-to-all-start = ((f32[256,1,512]{2,1,0:T(1,128)}), f32[256,1,512]{2,1,0:T(1,128)S(1)}, u32[]{:S(2)}, u32[]{:S(2)}) async-start(f32[256,1,512]{2,1,0:T(1,128)} %copy.18), calls=%async_computation | async-start | bytes 1048576 | tf_op jit(solution)/shard_map/all_to_all | solution.py:116
  29.1 21.3 %copy-start.1 = (f32[512,256]{1,0:T(8,128)S(1)}, f32[512,256]{1,0:T(8,128)}, u32[]{:S(2)}) copy-start(f32[512,256]{1,0:T(8,128)} %constant.21.clone.table_ref) | copy-start | bytes 1572868
  29.1 21.3 %copy-start.2 = (f32[256,128]{1,0:T(8,128)S(1)}, f32[256,128]{1,0:T(8,128)}, u32[]{:S(2)}) copy-start(f32[256,128]{1,0:T(8,128)} %constant.20.clone.rows_ref) | copy-start | bytes 393220

commit v3 on v2

--- a/solution.py
+++ b/solution.py
@@ -44,15 +44,10 @@
     return product(left_high, right_high) + small
 
 
-def convolve_kernel(place_ref, signal_ref, rows_ref, table_ref, out_ref, mix_ref):
+def convolve_kernel(place_ref, signal_ref, rows_ref, table_ref, out_ref):
     n = SIDE
-    own = pl.ds(pl.multiple_of(place_ref[0] * n, n), n)
-    share = pl.multiple_of(place_ref[1] * SHARE, SHARE)
-    grad_mix = signal_ref[:n, :n] + signal_ref[n:, :n]
-    mix_ref[...] = grad_mix
-    grad_conv = (grad_mix * signal_ref[own, 3 * n :]).astype(jnp.bfloat16)
-    others = signal_ref[own, n : 3 * n].astype(jnp.bfloat16)
-    signals = jnp.concatenate([grad_conv, others], axis=1)
+    share = pl.multiple_of(place_ref[0] * SHARE, SHARE)
+    signals = signal_ref[...].astype(jnp.bfloat16)
     rows_high, rows_low = split(rows_ref[...])
     spread = product(rows_high, signals) + product(rows_low, signals)
     columns = split(table_ref[: 2 * n, :])
@@ -78,8 +73,7 @@
         turned.append(jnp.concatenate([re * cos + im * sin, re * sin - im * cos], axis=0))
     last = split(table_ref[pl.ds(2 * n + share, SHARE), :])
     results = wide_product(last, split(jnp.concatenate(turned, axis=1))) * (1.0 / LENGTH)
-    out_ref[:, :n] = results[:, :n] * mix_ref[pl.ds(share, SHARE), :]
-    out_ref[:, n:] = results[:, n:]
+    out_ref[...] = results
 
 
 def convolve(place, signals):
@@ -90,7 +84,6 @@
         in_specs=[pl.BlockSpec(memory_space=pltpu.SMEM)]
         + [pl.BlockSpec(memory_space=pltpu.VMEM)] * 3,
         out_specs=pl.BlockSpec(memory_space=pltpu.VMEM),
-        scratch_shapes=[pltpu.VMEM((SIDE, SIDE), jnp.float32)],
         compiler_params=pltpu.CompilerParams(vmem_limit_bytes=32 * 1024 * 1024),
         cost_estimate=pl.CostEstimate(
             flops=400_000_000, bytes_accessed=1_200_000, transcendentals=0
@@ -111,22 +104,25 @@
     kept = jnp.where(core == 0, partial[:, 0], partial[:, 1])
     sent = jnp.where(core == 0, partial[:, 1], partial[:, 0])
     partial = kept + lax.ppermute(sent, "core", [(0, 1), (1, 0)])
-    own = [gated, taps, outer]
-    signals = [jnp.concatenate([partial[to], *own], axis=1) for to in range(2) for _ in range(4)]
+    kept = jnp.where(half == 0, partial[0], partial[1])
+    sent = jnp.where(half == 0, partial[1], partial[0])
+    grad_mix = kept + lax.ppermute(sent, "z_hi", [(0, 1), (1, 0)])
+    grad_conv = (grad_mix * outer).astype(jnp.bfloat16).astype(jnp.float32)
+    signals = jnp.concatenate([grad_conv, gated, taps], axis=1)
     signals = lax.all_to_all(
-        jnp.concatenate(signals, axis=0), ("z_hi",) + SEQ, split_axis=0, concat_axis=0, tiled=True
+        jnp.concatenate([signals] * 4, axis=0), SEQ, split_axis=0, concat_axis=0, tiled=True
     )
-    place = jnp.stack([half, lax.axis_index("y_hi")]).astype(jnp.int32)
+    place = lax.axis_index("y_hi").astype(jnp.int32).reshape(1)
     results = convolve(place, signals)
     results = lax.all_to_all(results, OWNERS, split_axis=0, concat_axis=0, tiled=True)
-    grad_outgate, grad_input, grad_taps = (
+    conv, grad_input, grad_taps = (
         results[:, :SIDE],
         results[:, SIDE : 2 * SIDE],
         results[:, 2 * SIDE :],
     )
     grad_gate = (grad_input * value).astype(jnp.bfloat16)
     grad_value = (grad_input * gate).astype(jnp.bfloat16)
-    return (grad_gate, grad_value, grad_outgate.astype(jnp.bfloat16), grad_taps * LENGTH**-0.5)
+    return (grad_gate, grad_value, (grad_mix * conv).astype(jnp.bfloat16), grad_taps * LENGTH**-0.5)
 
 
 def solution(mesh):

time: 66.7 us -> 61 us (0.915)
  waiting for transfers between devices: 21.7 us -> 15.4 us
  starting transfers between devices: 23.3 us -> 26.9 us
  local copies, waits for them, and re-layouts: 3.77 us -> 2.03 us
    ppermute x0 -> x1, starting transfers between devices: none -> 10.9 us  [local(): grad_mix = kept + lax.ppermute(sent, 'z_hi', [(0, 1), (1, 0)])]
    all_to_all x1, waiting for transfers between devices: 21.3 us -> 12.6 us  [local(): lax.all_to_all(jnp.concatenate([signals] * 4, axis=0), SEQ, split_axis=0,...]
    all_to_all x1, starting transfers between devices: 21.3 us -> 14.1 us  [local(): lax.all_to_all(jnp.concatenate([signals] * 4, axis=0), SEQ, split_axis=0,...]
    ppermute x0 -> x1, waiting for transfers between devices: none -> 1.66 us  [local(): grad_mix = kept + lax.ppermute(sent, 'z_hi', [(0, 1), (1, 0)])]
    ppermute x1, waiting for transfers between devices: 0.43 us -> 1.17 us  [local(): partial = kept + lax.ppermute(sent, 'core', [(0, 1), (1, 0)])]
    unnamed x16, local copies, waits for them, and re-layouts: 1.78 us -> 1.09 us
  transfers between devices with their start and end apart: 2 -> 3, of which waited for: 2 -> 3; matrix products, arithmetic and copies ran while one was open for 0% -> 0% of each run, Pallas kernels for 0% -> 0%
where the time goes in v3:
time: 61 us; the launch traced here: 60.6 us
  starting transfers between devices  26.9 us (44%)
  waiting for transfers between devices  15.4 us (25%)
  blocking collectives  12.1 us (20%)
  local copies, waits for them, and re-layouts  2.03 us (3%)
  matrix products  1.34 us (2%)
  Pallas kernels  1.27 us (2%)
  between operations  0.83 us (1%)
  other arithmetic  0.68 us (1%)
    all_to_all x1, starting transfers between devices, local(): lax.all_to_all(jnp.concatenate([signals] * 4, axis=0), SEQ, split_axis=0,...  14.1 us
    all_to_all x1, waiting for transfers between devices, local(): lax.all_to_all(jnp.concatenate([signals] * 4, axis=0), SEQ, split_axis=0,...  12.6 us
    all_to_all x1, blocking collectives, local(): lax.all_to_all(results, OWNERS, split_axis=0, concat_axis=0, tiled=True)  12.1 us
    ppermute x1, starting transfers between devices, local(): grad_mix = kept + lax.ppermute(sent, 'z_hi', [(0, 1), (1, 0)])  10.9 us
    ppermute x1, starting transfers between devices, local(): partial = kept + lax.ppermute(sent, 'core', [(0, 1), (1, 0)])  1.92 us
    ppermute x1, waiting for transfers between devices, local(): grad_mix = kept + lax.ppermute(sent, 'z_hi', [(0, 1), (1, 0)])  1.66 us
    dot_general x1, matrix products, local(): lax.dot_general(out_weight, out_grad, (((1,), (1,)), ((), ())), preferred...  1.34 us
    pallas_call x1, Pallas kernels, convolve(): pl.pallas_call(convolve_kernel, out_shape=jax.ShapeDtypeStruct((SHARE, 3...  1.27 us
  transfers between devices with their start and end apart: 3, of which 3 were waited for; matrix products, arithmetic and copies ran while one was open for 0% of the time, Pallas kernels for 0%

profile of v3, /device:TPU:8, one launch (start us, length us, event | category | flops | bytes accessed | tf_op | source)
XLA Modules:
  0.0 60.6 jit_solution(2642837456757573446)
XLA Ops:
  0.6 0.0 copy-start
  0.7 1.0 %copy-done = bf16[128,2048]{1,0:T(8,128)(2,1)S(1)} copy-done((bf16[128,2048]{1,0:T(8,128)(2,1)S(1)}, bf16[128,2048]{1,0:T(8,128)(2,1)}, u32[]{:S(2)}) %copy-start) | copy-done | bytes 524312
  1.7 1.3 %fusion.7 = f32[128,128]{1,0:T(8,128)S(1)} fusion(bf16[128,2048]{1,0:T(8,128)(2,1)S(1)} %copy-done, bf16[128,2048]{1,0:T(8,128)(2,1)} %param.13), kind=kOutput, calls=%fused_computation.20 | convolution fusion | flops 67108864 | bytes 1114112 | tf_op jit(solution)/shard_map/dot_general | solution.py:100
  3.0 1.9 %collective-permute-start = (f32[2,32,128]{2,1,0:T(8,128)S(1)}, f32[2,32,128]{2,1,0:T(8,128)S(1)}, u32[]{:S(2)}, u32[]{:S(2)}) collective-permute-start(f32[2,32,128]{2,1,0:T(8,128)S(1)} %select_bitcast_fusion), channel_id=1, source_target_pairs={{0,1},{1,0},{2,3},{3,2},{4,5},{5,4},{6,7},{7,6},{8,9},{9,8},{10,11... | collective-permute-start | bytes 98312 | tf_op jit(solution)/shard_map/ppermute | solution.py:106
  5.0 1.2 %collective-permute-done = f32[2,32,128]{2,1,0:T(8,128)S(1)} collective-permute-done((f32[2,32,128]{2,1,0:T(8,128)S(1)}, f32[2,32,128]{2,1,0:T(8,128)S(1)}, u32[]{:S(2)}, u32[]{:S(2)}) %collective-permute-start) | collective-permute-done | bytes 32800 | tf_op jit(solution)/shard_map/ppermute | solution.py:106
  6.2 0.0 copy-start.3
  6.2 0.0 copy-start.4
  6.2 0.0 copy-start.6
  6.2 10.9 %collective-permute-start.1 = (f32[32,128]{1,0:T(8,128)S(1)}, f32[32,128]{1,0:T(8,128)S(1)}, u32[]{:S(2)}, u32[]{:S(2)}) collective-permute-start(f32[32,128]{1,0:T(8,128)S(1)} %select_bitcast_fusion.1), channel_id=1, source_target_pairs={{0,2},{2,0},{1,3},{3,1},{4,6},{6,4},{5,7},{7,5},{8,10},{10,8},{9,1... | collective-permute-start | bytes 49160 | tf_op jit(solution)/shard_map/ppermute | solution.py:109
  17.1 0.0 copy-done.3
  17.1 0.0 copy-done.4
  17.2 0.0 copy-start.5
  17.2 1.7 %collective-permute-done.1 = f32[32,128]{1,0:T(8,128)S(1)} collective-permute-done((f32[32,128]{1,0:T(8,128)S(1)}, f32[32,128]{1,0:T(8,128)S(1)}, u32[]{:S(2)}, u32[]{:S(2)}) %collective-permute-start.1) | collective-permute-done | bytes 16416 | tf_op jit(solution)/shard_map/ppermute | solution.py:109
  18.8 0.0 copy-done.6
  18.8 0.0 copy-done.5
  18.9 0.0 copy-start.1
  18.9 0.9 %copy.18 = f32[128,1,384]{2,1,0:T(1,128)} copy(f32[128,1,384]{2,0,1:T(8,128)S(1)} %fusion) | data formatting | bytes 393216 | tf_op jit(solution)/shard_map/all_to_all | solution.py:112
  19.8 14.1 %all-to-all-start = ((f32[128,1,384]{2,1,0:T(1,128)}), f32[128,1,384]{2,1,0:T(1,128)S(1)}, u32[]{:S(2)}, u32[]{:S(2)}) async-start(f32[128,1,384]{2,1,0:T(1,128)} %copy.18), calls=%async_computation | async-start | bytes 393216 | tf_op jit(solution)/shard_map/all_to_all | solution.py:112
  33.9 0.0 copy-start.2
  33.9 12.6 %all-to-all-done = f32[128,1,384]{2,1,0:T(1,128)S(1)} async-done(((f32[128,1,384]{2,1,0:T(1,128)}), f32[128,1,384]{2,1,0:T(1,128)S(1)}, u32[]{:S(2)}, u32[]{:S(2)}) %all-to-all-start) | async-done | bytes 196640 | tf_op jit(solution)/shard_map/all_to_all | solution.py:112
  46.5 1.3 %convolve.1 = f32[32,384]{1,0:T(8,128)S(1)} custom-call(s32[1]{0:T(128)} %bitcast.place_ref, f32[128,384]{1,0:T(8,128)S(1)} %bitcast.39, f32[256,128]{1,0:T(8,128)S(1)} %copy-done.2, f32[512,256]{1,0:T(8,128)S(1)} %copy-done.1), custom_call_target="tpu_custom_call" | custom-call | flops 400000000 | bytes 1200000 | tf_op jit(solution)/shard_map/convolve/pallas_call | solution.py:81
  47.8 0.1 copy.19
  47.9 12.1 %all_to_all.27 = f32[32,1,384]{2,1,0:T(1,128)S(1)} all-to-all(f32[32,1,384]{2,1,0:T(1,128)S(1)} %copy.19), channel_id=1, replica_groups=mesh['y_hi'=4,'y_lo'=2,'z'=4,'x'=4,'z_hi'=2,'core'=2] {'y_lo','z','x'}, dimensions={0} | all-to-all | bytes 98304 | tf_op jit(solution)/shard_map/all_to_all | solution.py:117
  60.0 0.6 %slice_multiply_fusion = (f32[32,128]{1,0:T(8,128)}, bf16[32,128]{1,0:T(8,128)(2,1)}, bf16[32,128]{1,0:T(8,128)(2,1)}, bf16[32,128]{1,0:T(8,128)(2,1)}) fusion(f32[32,384]{1,0:T(8,128)S(1)} %bitcast.43, bf16[32,128]{1,0:T(8,128)(2,1)S(1)} %copy-done.4, f32[32,128]{1,0:T(8,128)S(1)} %get-tuple-element.5, bf16[32,128]{1,0:T(8,128)(2,1)S(1)} %copy-done.3), kind=kLoop, calls=%fused_computation.14 | loop fusion | flops 36864 | bytes 122880 | tf_op jit(solution)/shard_map/mul | solution.py:125
  (10 shorter events, 0.1 us)
Async XLA Ops:
  0.6 1.0 %copy-start = (bf16[128,2048]{1,0:T(8,128)(2,1)S(1)}, bf16[128,2048]{1,0:T(8,128)(2,1)}, u32[]{:S(2)}) copy-start(bf16[128,2048]{1,0:T(8,128)(2,1)} %param.12) | copy-start | bytes 1572868
  3.0 3.1 %collective-permute-start = (f32[2,32,128]{2,1,0:T(8,128)S(1)}, f32[2,32,128]{2,1,0:T(8,128)S(1)}, u32[]{:S(2)}, u32[]{:S(2)}) collective-permute-start(f32[2,32,128]{2,1,0:T(8,128)S(1)} %select_bitcast_fusion), channel_id=1, source_target_pairs={{0,1},{1,0},{2,3},{3,2},{4,5},{5,4},{6,7},{7,6},{8,9},{9,8},{10,11... | collective-permute-start | bytes 98312 | tf_op jit(solution)/shard_map/ppermute | solution.py:106
  6.2 11.0 %copy-start.3 = (bf16[32,128]{1,0:T(8,128)(2,1)S(1)}, bf16[32,128]{1,0:T(8,128)(2,1)}, u32[]{:S(2)}) copy-start(bf16[32,128]{1,0:T(8,128)(2,1)} %param.9) | copy-start | bytes 24580
  6.2 11.0 %copy-start.4 = (bf16[32,128]{1,0:T(8,128)(2,1)S(1)}, bf16[32,128]{1,0:T(8,128)(2,1)}, u32[]{:S(2)}) copy-start(bf16[32,128]{1,0:T(8,128)(2,1)} %param.8) | copy-start | bytes 24580
  6.2 12.6 %copy-start.6 = (bf16[32,128]{1,0:T(8,128)(2,1)S(1)}, bf16[32,128]{1,0:T(8,128)(2,1)}, u32[]{:S(2)}) copy-start(bf16[32,128]{1,0:T(8,128)(2,1)} %param.10) | copy-start | bytes 24580
  6.2 12.6 %collective-permute-start.1 = (f32[32,128]{1,0:T(8,128)S(1)}, f32[32,128]{1,0:T(8,128)S(1)}, u32[]{:S(2)}, u32[]{:S(2)}) collective-permute-start(f32[32,128]{1,0:T(8,128)S(1)} %select_bitcast_fusion.1), channel_id=1, source_target_pairs={{0,2},{2,0},{1,3},{3,1},{4,6},{6,4},{5,7},{7,5},{8,10},{10,8},{9,1... | collective-permute-start | bytes 49160 | tf_op jit(solution)/shard_map/ppermute | solution.py:109
  17.2 1.7 %copy-start.5 = (bf16[32,128]{1,0:T(8,128)(2,1)S(1)}, bf16[32,128]{1,0:T(8,128)(2,1)}, u32[]{:S(2)}) copy-start(bf16[32,128]{1,0:T(8,128)(2,1)} %param.11) | copy-start | bytes 24580
  18.9 27.6 %copy-start.1 = (f32[512,256]{1,0:T(8,128)S(1)}, f32[512,256]{1,0:T(8,128)}, u32[]{:S(2)}) copy-start(f32[512,256]{1,0:T(8,128)} %constant.21.clone.table_ref) | copy-start | bytes 1572868
  19.8 26.7 %all-to-all-start = ((f32[128,1,384]{2,1,0:T(1,128)}), f32[128,1,384]{2,1,0:T(1,128)S(1)}, u32[]{:S(2)}, u32[]{:S(2)}) async-start(f32[128,1,384]{2,1,0:T(1,128)} %copy.18), calls=%async_computation | async-start | bytes 393216 | tf_op jit(solution)/shard_map/all_to_all | solution.py:112
  33.9 12.6 %copy-start.2 = (f32[256,128]{1,0:T(8,128)S(1)}, f32[256,128]{1,0:T(8,128)}, u32[]{:S(2)}) copy-start(f32[256,128]{1,0:T(8,128)} %constant.20.clone.rows_ref) | copy-start | bytes 393220

commit v4 on v3

--- a/solution.py
+++ b/solution.py
@@ -10,6 +10,7 @@
 SIDE = 128
 SHARE = 32
 LENGTH = SIDE * SIDE
+CHUNKS = 2
 SEQ = ("y_hi", "y_lo", "z", "x")
 OWNERS = ("y_lo", "z", "x")
 CHAN = ("z_hi", "core")
@@ -92,17 +93,62 @@
     )(place, signals, jnp.asarray(rows), jnp.asarray(table))
 
 
+def mix_kernel(weight_hbm, grad_hbm, kept_ref, sent_ref, weight, grad, total, sems):
+    copies = []
+    for at in range(CHUNKS):
+        columns = pl.ds(at * (weight.shape[1] // CHUNKS), weight.shape[1] // CHUNKS)
+        pair = []
+        for number, (source, target) in enumerate(((weight_hbm, weight), (grad_hbm, grad))):
+            copy = pltpu.make_async_copy(
+                source.at[:, columns], target.at[:, columns], sems.at[number, at]
+            )
+            copy.start()
+            pair.append(copy)
+        copies.append((columns, pair))
+    partial = jnp.zeros(total.shape, jnp.float32)
+    for columns, pair in copies:
+        for copy in pair:
+            copy.wait()
+        partial = partial + lax.dot_general(
+            weight[:, columns],
+            grad[:, columns],
+            (((1,), (1,)), ((), ())),
+            preferred_element_type=jnp.float32,
+        )
+    total[...] = partial
+    channels = kept_ref.shape[1]
+    core = lax.axis_index("core")
+    for half in range(2):
+        own = pl.multiple_of((2 * half + core) * channels, channels)
+        other = pl.multiple_of((2 * half + 1 - core) * channels, channels)
+        kept_ref[half] = total[pl.ds(own, channels), :]
+        sent_ref[half] = total[pl.ds(other, channels), :]
+
+
+def partial_mix(weight, grad, channels):
+    return pl.pallas_call(
+        mix_kernel,
+        out_shape=[jax.ShapeDtypeStruct((2, channels, SIDE), jnp.float32)] * 2,
+        in_specs=[pl.BlockSpec(memory_space=pltpu.HBM)] * 2,
+        out_specs=[pl.BlockSpec(memory_space=pltpu.VMEM)] * 2,
+        scratch_shapes=[
+            pltpu.VMEM(weight.shape, weight.dtype),
+            pltpu.VMEM(grad.shape, grad.dtype),
+            pltpu.VMEM((4 * channels, SIDE), jnp.float32),
+            pltpu.SemaphoreType.DMA((2, CHUNKS)),
+        ],
+        compiler_params=pltpu.CompilerParams(vmem_limit_bytes=int(53.6 * 1024 * 1024)),
+        name="partial_mix",
+    )(weight, grad)
+
+
 def local(gate_in, value_in, out_gate, filter_taps, out_weight, out_grad):
-    channels, tok_rows = gate_in.shape
+    channels = gate_in.shape[0]
     gate, value = gate_in.astype(jnp.float32), value_in.astype(jnp.float32)
     gated = (gate * value).astype(jnp.bfloat16).astype(jnp.float32)
     taps, outer = filter_taps.astype(jnp.float32), out_gate.astype(jnp.float32)
-    partial = lax.dot_general(
-        out_weight, out_grad, (((1,), (1,)), ((), ())), preferred_element_type=jnp.float32
-    ).reshape(2, 2, channels, tok_rows)
-    core, half = lax.axis_index("core"), lax.axis_index("z_hi")
-    kept = jnp.where(core == 0, partial[:, 0], partial[:, 1])
-    sent = jnp.where(core == 0, partial[:, 1], partial[:, 0])
+    half = lax.axis_index("z_hi")
+    kept, sent = partial_mix(out_weight, out_grad, channels)
     partial = kept + lax.ppermute(sent, "core", [(0, 1), (1, 0)])
     kept = jnp.where(half == 0, partial[0], partial[1])
     sent = jnp.where(half == 0, partial[1], partial[0])

time: 61 us -> 60.1 us (0.985)
  Pallas kernels: 1.27 us -> 2.81 us
  matrix products: 1.34 us -> 0 us
  local copies, waits for them, and re-layouts: 2.03 us -> 0.99 us
    pallas_call x0 -> x1, Pallas kernels: none -> 1.54 us  [partial_mix(): pl.pallas_call(mix_kernel, out_shape=[jax.ShapeDtypeStruct((2, channels,...]
    dot_general x1 -> x0, matrix products: 1.34 us -> none  [local(): lax.dot_general(out_weight, out_grad, (((1,), (1,)), ((), ())), preferred...]
    unnamed x16 -> x14, local copies, waits for them, and re-layouts: 1.09 us -> 0.05 us
where the time goes in v4:
time: 60.1 us; the launch traced here: 59.8 us
  starting transfers between devices  26.9 us (45%)
  waiting for transfers between devices  15.6 us (26%)
  blocking collectives  12.1 us (20%)
  Pallas kernels  2.81 us (5%)
  local copies, waits for them, and re-layouts  0.99 us (2%)
  between operations  0.8 us (1%)
  other arithmetic  0.67 us (1%)
    all_to_all x1, starting transfers between devices, local(): lax.all_to_all(jnp.concatenate([signals] * 4, axis=0), SEQ, split_axis=0,...  14.1 us
    all_to_all x1, waiting for transfers between devices, local(): lax.all_to_all(jnp.concatenate([signals] * 4, axis=0), SEQ, split_axis=0,...  12.8 us
    all_to_all x1, blocking collectives, local(): lax.all_to_all(results, OWNERS, split_axis=0, concat_axis=0, tiled=True)  12.1 us
    ppermute x1, starting transfers between devices, local(): grad_mix = kept + lax.ppermute(sent, 'z_hi', [(0, 1), (1, 0)])  10.9 us
    ppermute x1, starting transfers between devices, local(): partial = kept + lax.ppermute(sent, 'core', [(0, 1), (1, 0)])  1.92 us
    ppermute x1, waiting for transfers between devices, local(): grad_mix = kept + lax.ppermute(sent, 'z_hi', [(0, 1), (1, 0)])  1.66 us
    pallas_call x1, Pallas kernels, partial_mix(): pl.pallas_call(mix_kernel, out_shape=[jax.ShapeDtypeStruct((2, channels,...  1.54 us
    pallas_call x1, Pallas kernels, convolve(): pl.pallas_call(convolve_kernel, out_shape=jax.ShapeDtypeStruct((SHARE, 3...  1.27 us
  transfers between devices with their start and end apart: 3, of which 3 were waited for; matrix products, arithmetic and copies ran while one was open for 0% of the time, Pallas kernels for 0%

profile of v4, /device:TPU:8, one launch (start us, length us, event | category | flops | bytes accessed | tf_op | source)
XLA Modules:
  0.0 59.8 jit_solution(4252149148966417257)
XLA Ops:
  0.6 1.5 %partial_mix.1 = (f32[2,32,128]{2,1,0:T(8,128)S(1)}, f32[2,32,128]{2,1,0:T(8,128)S(1)}) custom-call(bf16[128,2048]{1,0:T(8,128)(2,1)} %weight_hbm.1, bf16[128,2048]{1,0:T(8,128)(2,1)} %grad_hbm.1), custom_call_target="tpu_custom_call" | custom-call | tf_op jit(solution)/shard_map/partial_mix/pallas_call | solution.py:129
  2.2 1.9 %collective-permute-start = (f32[2,32,128]{2,1,0:T(8,128)S(1)}, f32[2,32,128]{2,1,0:T(8,128)S(1)}, u32[]{:S(2)}, u32[]{:S(2)}) collective-permute-start(f32[2,32,128]{2,1,0:T(8,128)S(1)} %get-tuple-element.7), channel_id=1, source_target_pairs={{0,1},{1,0},{2,3},{3,2},{4,5},{5,4},{6,7},{7,6},{8,9},{9,8},{10,11... | collective-permute-start | bytes 98312 | tf_op jit(solution)/shard_map/ppermute | solution.py:152
  4.1 1.2 %collective-permute-done = f32[2,32,128]{2,1,0:T(8,128)S(1)} collective-permute-done((f32[2,32,128]{2,1,0:T(8,128)S(1)}, f32[2,32,128]{2,1,0:T(8,128)S(1)}, u32[]{:S(2)}, u32[]{:S(2)}) %collective-permute-start) | collective-permute-done | bytes 32800 | tf_op jit(solution)/shard_map/ppermute | solution.py:152
  5.3 0.0 copy-start.2
  5.3 0.0 copy-start.3
  5.3 0.0 copy-start.5
  5.3 10.9 %collective-permute-start.1 = (f32[32,128]{1,0:T(8,128)S(1)}, f32[32,128]{1,0:T(8,128)S(1)}, u32[]{:S(2)}, u32[]{:S(2)}) collective-permute-start(f32[32,128]{1,0:T(8,128)S(1)} %select_bitcast_fusion), channel_id=1, source_target_pairs={{0,2},{2,0},{1,3},{3,1},{4,6},{6,4},{5,7},{7,5},{8,10},{10,8},{9,1... | collective-permute-start | bytes 49160 | tf_op jit(solution)/shard_map/ppermute | solution.py:155
  16.3 0.0 copy-done.2
  16.3 0.0 copy-done.3
  16.3 0.0 copy-start.4
  16.3 1.7 %collective-permute-done.1 = f32[32,128]{1,0:T(8,128)S(1)} collective-permute-done((f32[32,128]{1,0:T(8,128)S(1)}, f32[32,128]{1,0:T(8,128)S(1)}, u32[]{:S(2)}, u32[]{:S(2)}) %collective-permute-start.1) | collective-permute-done | bytes 16416 | tf_op jit(solution)/shard_map/ppermute | solution.py:155
  18.0 0.0 copy-done.5
  18.0 0.0 copy-done.4
  18.0 0.0 copy-start
  18.0 0.9 %copy.12 = f32[128,1,384]{2,1,0:T(1,128)} copy(f32[128,1,384]{2,0,1:T(8,128)S(1)} %fusion) | data formatting | bytes 393216 | tf_op jit(solution)/shard_map/all_to_all | solution.py:158
  18.9 14.1 %all-to-all-start = ((f32[128,1,384]{2,1,0:T(1,128)}), f32[128,1,384]{2,1,0:T(1,128)S(1)}, u32[]{:S(2)}, u32[]{:S(2)}) async-start(f32[128,1,384]{2,1,0:T(1,128)} %copy.12), calls=%async_computation | async-start | bytes 393216 | tf_op jit(solution)/shard_map/all_to_all | solution.py:158
  33.0 0.0 copy-start.1
  33.0 12.8 %all-to-all-done = f32[128,1,384]{2,1,0:T(1,128)S(1)} async-done(((f32[128,1,384]{2,1,0:T(1,128)}), f32[128,1,384]{2,1,0:T(1,128)S(1)}, u32[]{:S(2)}, u32[]{:S(2)}) %all-to-all-start) | async-done | bytes 196640 | tf_op jit(solution)/shard_map/all_to_all | solution.py:158
  45.8 0.0 copy-done
  45.8 0.0 copy-done.1
  45.8 1.3 %convolve.1 = f32[32,384]{1,0:T(8,128)S(1)} custom-call(s32[1]{0:T(128)} %bitcast.place_ref, f32[128,384]{1,0:T(8,128)S(1)} %bitcast.18, f32[256,128]{1,0:T(8,128)S(1)} %copy-done.1, f32[512,256]{1,0:T(8,128)S(1)} %copy-done), custom_call_target="tpu_custom_call" | custom-call | flops 400000000 | bytes 1200000 | tf_op jit(solution)/shard_map/convolve/pallas_call | solution.py:82
  47.1 0.1 copy.13
  47.1 12.1 %all_to_all.27 = f32[32,1,384]{2,1,0:T(1,128)S(1)} all-to-all(f32[32,1,384]{2,1,0:T(1,128)S(1)} %copy.13), channel_id=1, replica_groups=mesh['y_hi'=4,'y_lo'=2,'z'=4,'x'=4,'z_hi'=2,'core'=2] {'y_lo','z','x'}, dimensions={0} | all-to-all | bytes 98304 | tf_op jit(solution)/shard_map/all_to_all | solution.py:163
  59.2 0.6 %slice_multiply_fusion = (f32[32,128]{1,0:T(8,128)}, bf16[32,128]{1,0:T(8,128)(2,1)}, bf16[32,128]{1,0:T(8,128)(2,1)}, bf16[32,128]{1,0:T(8,128)(2,1)}) fusion(f32[32,384]{1,0:T(8,128)S(1)} %bitcast.20, bf16[32,128]{1,0:T(8,128)(2,1)S(1)} %copy-done.3, f32[32,128]{1,0:T(8,128)S(1)} %get-tuple-element.9, bf16[32,128]{1,0:T(8,128)(2,1)S(1)} %copy-done.2), kind=kLoop, calls=%fused_computation.10 | loop fusion | flops 36864 | bytes 122880 | tf_op jit(solution)/shard_map/mul | solution.py:171
  (7 shorter events, 0.1 us)
Async XLA Ops:
  2.2 3.1 %collective-permute-start = (f32[2,32,128]{2,1,0:T(8,128)S(1)}, f32[2,32,128]{2,1,0:T(8,128)S(1)}, u32[]{:S(2)}, u32[]{:S(2)}) collective-permute-start(f32[2,32,128]{2,1,0:T(8,128)S(1)} %get-tuple-element.7), channel_id=1, source_target_pairs={{0,1},{1,0},{2,3},{3,2},{4,5},{5,4},{6,7},{7,6},{8,9},{9,8},{10,11... | collective-permute-start | bytes 98312 | tf_op jit(solution)/shard_map/ppermute | solution.py:152
  5.3 11.0 %copy-start.2 = (bf16[32,128]{1,0:T(8,128)(2,1)S(1)}, bf16[32,128]{1,0:T(8,128)(2,1)}, u32[]{:S(2)}) copy-start(bf16[32,128]{1,0:T(8,128)(2,1)} %param.9) | copy-start | bytes 24580
  5.3 11.0 %copy-start.3 = (bf16[32,128]{1,0:T(8,128)(2,1)S(1)}, bf16[32,128]{1,0:T(8,128)(2,1)}, u32[]{:S(2)}) copy-start(bf16[32,128]{1,0:T(8,128)(2,1)} %param.8) | copy-start | bytes 24580
  5.3 12.6 %copy-start.5 = (bf16[32,128]{1,0:T(8,128)(2,1)S(1)}, bf16[32,128]{1,0:T(8,128)(2,1)}, u32[]{:S(2)}) copy-start(bf16[32,128]{1,0:T(8,128)(2,1)} %param.10) | copy-start | bytes 24580
  5.3 12.6 %collective-permute-start.1 = (f32[32,128]{1,0:T(8,128)S(1)}, f32[32,128]{1,0:T(8,128)S(1)}, u32[]{:S(2)}, u32[]{:S(2)}) collective-permute-start(f32[32,128]{1,0:T(8,128)S(1)} %select_bitcast_fusion), channel_id=1, source_target_pairs={{0,2},{2,0},{1,3},{3,1},{4,6},{6,4},{5,7},{7,5},{8,10},{10,8},{9,1... | collective-permute-start | bytes 49160 | tf_op jit(solution)/shard_map/ppermute | solution.py:155
  16.3 1.7 %copy-start.4 = (bf16[32,128]{1,0:T(8,128)(2,1)S(1)}, bf16[32,128]{1,0:T(8,128)(2,1)}, u32[]{:S(2)}) copy-start(bf16[32,128]{1,0:T(8,128)(2,1)} %param.11) | copy-start | bytes 24580
  18.0 27.8 %copy-start = (f32[512,256]{1,0:T(8,128)S(1)}, f32[512,256]{1,0:T(8,128)}, u32[]{:S(2)}) copy-start(f32[512,256]{1,0:T(8,128)} %constant.19.clone.table_ref) | copy-start | bytes 1572868
  18.9 26.9 %all-to-all-start = ((f32[128,1,384]{2,1,0:T(1,128)}), f32[128,1,384]{2,1,0:T(1,128)S(1)}, u32[]{:S(2)}, u32[]{:S(2)}) async-start(f32[128,1,384]{2,1,0:T(1,128)} %copy.12), calls=%async_computation | async-start | bytes 393216 | tf_op jit(solution)/shard_map/all_to_all | solution.py:158
  33.0 12.8 %copy-start.1 = (f32[256,128]{1,0:T(8,128)S(1)}, f32[256,128]{1,0:T(8,128)}, u32[]{:S(2)}) copy-start(f32[256,128]{1,0:T(8,128)} %constant.18.clone.rows_ref) | copy-start | bytes 393220
